TPU v7x, 128 devices: a whole 4x4x4 slice. The times are simulated.
128 devices in a mesh: wide: 16 (over y, x_lo, core), narrow: 8 (over z, x_hi).
Axes of the slice: x: 4 (x_hi: 2, x_lo: 2; x = x_hi * 2 + x_lo), y: 4, z: 4, core: 2. Of those that a mesh axis runs over, the one named last changes fastest.
Arguments:
- interior: bfloat16 [16384, 65536], P('wide', 'narrow'), may hold values from -0.375 to 0.375
- tile_mask: int32 [256, 1024], P('wide', 'narrow'), may hold values 0 or 1
- owner: int32 [2], replicated, may hold values from 0 to 127
- stiffness: float32 [2, 512, 65536], P(None, 'wide', 'narrow'), may hold values from -4 to 4
Outputs:
- complement: float32 [2, 512, 65536], P(None, 'wide', 'narrow')
All inputs are finite; a program needn't handle non-finite values. No bound on the sum of `tile_mask` on one device may be relied on, other than what follows from the above.
Results may differ from a plain program's by a relative error of at most 0.0003.
Values may be sent and summed in bfloat16 or wider, within the bound.
A program may use at most 192 MiB of HBM per device.

v0:
```python
import jax
import jax.numpy as jnp
from jax import lax
from jax.sharding import PartitionSpec as P

PW = 512
STEPS = 2


def from_root(block, axis, source):
    block = jnp.where(lax.axis_index(axis) == source, block, jnp.zeros_like(block))
    return lax.psum(block, axis)


def scattered(portion, width, axis):
    count = width * lax.axis_size(axis)
    return lax.psum_scatter(portion(jnp.int32(0), count), axis, scatter_dimension=0, tiled=True)


def shards(interior, tile_mask, owner, stiffness):
    rows_here, cols_here = interior.shape
    tiled = (
        interior.reshape(rows_here // 64, 64, cols_here // 64, 64)
        * tile_mask.astype(jnp.bfloat16)[:, None, :, None]
    )
    masked = tiled.reshape(rows_here, cols_here)
    row_share = stiffness.shape[1]

    def product(panel_cols):
        return lax.dot_general(
            panel_cols, masked, (((0,), (0,)), ((), ())), preferred_element_type=jnp.float32
        )

    results = []
    for step_index in range(STEPS):
        first_col = owner[step_index] * PW
        holder = first_col // cols_here
        local_cols = lax.dynamic_slice_in_dim(masked, first_col % cols_here, PW, 1)
        panel_cols = from_root(local_cols, "narrow", holder)
        summed = scattered(
            lambda begin_row, row_count, held=panel_cols: product(held), row_share, "wide"
        )
        results.append(stiffness[step_index] - summed)
    return jnp.stack(results)


def solution(mesh):
    placed = (P("wide", "narrow"), P("wide", "narrow"), P(), P(None, "wide", "narrow"))
    return jax.shard_map(
        shards, mesh=mesh, in_specs=placed, out_specs=P(None, "wide", "narrow"), check_vma=False
    )
```

profile of v0, /device:TPU:0, one launch (start us, length us, event | category | flops | bytes accessed | tf_op | source)
XLA Modules:
  0.0 588.0 jit_solution(17429800776545964323)
XLA Ops:
  6.5 0.0 all-reduce.3.cloned.1.call-start
  6.5 1.3 fusion.2
  9.1 0.7 convert_element_type.3
  9.8 11.3 %mul.25 = bf16[16,64,128,64]{3,2,1,0:T(8,128)(2,1)} broadcast(bf16[16,128]{1,0:T(8,128)(2,1)S(1)} %convert_element_type.3), dimensions={0,2} | broadcast | bytes 16781312 | tf_op jit(solution)/shard_map/mul | solution.py:23
  21.1 44.0 %mul.26 = bf16[1024,8192]{1,0:T(8,128)(2,1)} reshape(bf16[16,64,128,64]{3,2,1,0:T(8,128)(2,1)} %mul.25) | data formatting | bytes 33554432 | tf_op jit(solution)/shard_map/mul | solution.py:23
  65.1 18.2 %mul.27 = bf16[1024,8192]{1,0:T(8,128)(2,1)} multiply(bf16[1024,8192]{1,0:T(8,128)(2,1)} %param.4, bf16[1024,8192]{1,0:T(8,128)(2,1)} %mul.26) | non-fusion elementwise | flops 8388608 | bytes 50331648 | tf_op jit(solution)/shard_map/mul | solution.py:23
  83.4 4.4 dynamic-slice_select_fusion.1
  87.7 0.0 all-reduce.3.cloned.1.call-update
  87.8 0.0 reduce-scatter.3.cloned.1.call-start
  87.8 110.2 %all-reduce.3.cloned.1.call-done = (bf16[1024,512]{1,0:T(8,128)(2,1)}, bf16[1024,512]{1,0:T(8,128)(2,1)}) async-done(((bf16[1024,512]{1,0:T(8,128)(2,1)}, bf16[1024,512]{1,0:T(8,128)(2,1)}), (bf16[1024,512]{1,0:T(8,128)(2,1)}, bf16[1024,512]{1,0:T(8,128)(2,1)})) %all-reduce.3.cloned.1.call-update) | async-done | bytes 2097168 | tf_op jit(solution)/shard_map/psum | solution.py:12
  198.0 16.0 %fusion.3 = f32[512,8192]{1,0:T(8,128)} fusion(bf16[1024,512]{1,0:T(8,128)(2,1)} %get-tuple-element.6, bf16[1024,8192]{1,0:T(8,128)(2,1)} %mul.27), kind=kOutput, calls=%fused_computation.8 | convolution fusion | flops 8589934592 | bytes 34603008 | tf_op jit(solution)/shard_map/dot_general | solution.py:30
  214.0 0.0 copy-start
  214.0 0.0 reduce-scatter.3.cloned.1.call-update
  214.1 0.2 reduce-scatter.5.cloned.1.call-start
  214.3 1.0 copy-done
  215.3 15.8 %fusion.4 = f32[512,8192]{1,0:T(8,128)} fusion(bf16[1024,512]{1,0:T(8,128)(2,1)S(1)} %copy-done, bf16[1024,8192]{1,0:T(8,128)(2,1)} %mul.27), kind=kOutput, calls=%fused_computation.9 | convolution fusion | flops 8589934592 | bytes 34603008 | tf_op jit(solution)/shard_map/dot_general | solution.py:30
  231.0 0.0 copy-start.1
  231.1 0.0 reduce-scatter.5.cloned.1.call-update
  231.1 163.7 %reduce-scatter.3.cloned.1.call-done = f32[32,8192]{1,0:T(8,128)} async-done(((f32[512,8192]{1,0:T(8,128)}), f32[32,8192]{1,0:T(8,128)}) %reduce-scatter.3.cloned.1.call-update) | async-done | bytes 1048592 | tf_op jit(solution)/shard_map/reduce_scatter | solution.py:17
  394.8 183.6 %reduce-scatter.5.cloned.1.call-done = f32[32,8192]{1,0:T(8,128)} async-done(((f32[512,8192]{1,0:T(8,128)}), f32[32,8192]{1,0:T(8,128)}) %reduce-scatter.5.cloned.1.call-update) | async-done | bytes 1048592 | tf_op jit(solution)/shard_map/reduce_scatter | solution.py:17
  578.4 0.0 copy-done.1
  578.4 3.1 fusion.1
  (1 shorter events, 0.0 us)
Async XLA Ops:
  6.5 191.5 %all-reduce.3.cloned.1.call-start = ((), (), s32[]{:S(2)}) async-start(), calls=%async_computation.4 | async-start | bytes 4194304 | tf_op jit(solution)/shard_map/psum | solution.py:12
  87.8 307.0 %reduce-scatter.3.cloned.1.call-start = ((), (), s32[]{:S(2)}) async-start(), calls=%async_computation.2 | async-start | bytes 17825792 | tf_op jit(solution)/shard_map/reduce_scatter | solution.py:17
  214.0 1.2 copy-start
  214.1 364.3 %reduce-scatter.5.cloned.1.call-start = ((), (), s32[]{:S(2)}) async-start(), calls=%async_computation.3 | async-start | bytes 17825792 | tf_op jit(solution)/shard_map/reduce_scatter | solution.py:17
  231.0 347.3 %copy-start.1 = (f32[2,32,8192]{2,1,0:T(8,128)S(1)}, f32[2,32,8192]{2,1,0:T(8,128)}, u32[]{:S(2)}) copy-start(f32[2,32,8192]{2,1,0:T(8,128)} %param.7) | copy-start | bytes 6291460
Sparse Core Ops, SparseCore 0:
  87.9 110.0 all-reduce.2
  214.2 180.5 reduce-scatter.2
  397.2 181.1 reduce-scatter.4
where the time goes:
time: 589 us; the launch traced here: 588 us
  waiting for transfers between devices  458 us (78%)
  local copies, waits for them, and re-layouts  57.6 us (10%)
  matrix products  31.8 us (5%)
  other arithmetic  26.4 us (4%)
  between operations  14.4 us (2%)
    reduce_scatter x2, waiting for transfers between devices, scattered(): lax.psum_scatter(portion(jnp.int32(0), count), axis, scatter_dimension=0,...  347 us
    psum x1, waiting for transfers between devices, from_root(): return lax.psum(block, axis)  110 us
    mul x2, local copies, waits for them, and re-layouts, shards(): interior.reshape(rows_here // 64, 64, cols_here // 64, 64)  55.3 us
    dot_general x2, matrix products, product(): lax.dot_general(panel_cols, masked, (((0,), (0,)), ((), ())), preferred_e...  31.8 us
    mul x1, other arithmetic, shards(): interior.reshape(rows_here // 64, 64, cols_here // 64, 64)  18.2 us
  transfers between devices with their start and end apart: 3, of which 3 were waited for; matrix products, arithmetic and copies ran while one was open for 3% of the time, Pallas kernels for 0%

commit v1 on v0

--- a/solution.py
+++ b/solution.py
@@ -9,7 +9,7 @@
 
 def from_root(block, axis, source):
     block = jnp.where(lax.axis_index(axis) == source, block, jnp.zeros_like(block))
-    return lax.psum(block, axis)
+    return jnp.sum(lax.all_gather(block, axis), axis=0)
 
 
 def scattered(portion, width, axis):

time: 589 us -> 682 us (1.16)
  waiting for transfers between devices: 458 us -> 541 us
  other arithmetic: 26.4 us -> 36.9 us
    all_gather x0 -> x2, waiting for transfers between devices: none -> 195 us  [from_root(): return jnp.sum(lax.all_gather(block, axis), axis=0)]
    psum x1 -> x0, waiting for transfers between devices: 110 us -> none  [from_root(): return lax.psum(block, axis)]
    reduce_sum x0 -> x2, other arithmetic: none -> 10.5 us  [from_root(): return jnp.sum(lax.all_gather(block, axis), axis=0)]
  transfers between devices with their start and end apart: 3 -> 4, of which waited for: 3 -> 4; matrix products, arithmetic and copies ran while one was open for 3% -> 6% of each run, Pallas kernels for 0% -> 0%
where the time goes in v1:
time: 682 us; the launch traced here: 681 us
  waiting for transfers between devices  541 us (79%)
  local copies, waits for them, and re-layouts  56.7 us (8%)
  other arithmetic  36.9 us (5%)
  matrix products  31.6 us (5%)
  between operations  14.5 us (2%)
    reduce_scatter x2, waiting for transfers between devices, scattered(): lax.psum_scatter(portion(jnp.int32(0), count), axis, scatter_dimension=0,...  345 us
    all_gather x2, waiting for transfers between devices, from_root(): return jnp.sum(lax.all_gather(block, axis), axis=0)  195 us
    mul x2, local copies, waits for them, and re-layouts, shards(): interior.reshape(rows_here // 64, 64, cols_here // 64, 64)  55.3 us
    dot_general x2, matrix products, product(): lax.dot_general(panel_cols, masked, (((0,), (0,)), ((), ())), preferred_e...  31.6 us
    mul x1, other arithmetic, shards(): interior.reshape(rows_here // 64, 64, cols_here // 64, 64)  18.2 us
  transfers between devices with their start and end apart: 4, of which 4 were waited for; matrix products, arithmetic and copies ran while one was open for 6% of the time, Pallas kernels for 0%

profile of v1, /device:TPU:0, one launch (start us, length us, event | category | flops | bytes accessed | tf_op | source)
XLA Modules:
  0.0 680.7 jit_solution(11209678567265354390)
XLA Ops:
  6.5 0.0 all-gather.5.cloned.1.call-start
  6.5 1.3 fusion.2
  9.2 0.7 convert_element_type.2
  9.9 11.3 %mul.25 = bf16[16,64,128,64]{3,2,1,0:T(8,128)(2,1)} broadcast(bf16[16,128]{1,0:T(8,128)(2,1)S(1)} %convert_element_type.2), dimensions={0,2} | broadcast | bytes 16781312 | tf_op jit(solution)/shard_map/mul | solution.py:23
  21.2 44.0 %mul.26 = bf16[1024,8192]{1,0:T(8,128)(2,1)} reshape(bf16[16,64,128,64]{3,2,1,0:T(8,128)(2,1)} %mul.25) | data formatting | bytes 33554432 | tf_op jit(solution)/shard_map/mul | solution.py:23
  65.2 18.2 %mul.27 = bf16[1024,8192]{1,0:T(8,128)(2,1)} multiply(bf16[1024,8192]{1,0:T(8,128)(2,1)} %param.4, bf16[1024,8192]{1,0:T(8,128)(2,1)} %mul.26) | non-fusion elementwise | flops 8388608 | bytes 50331648 | tf_op jit(solution)/shard_map/mul | solution.py:23
  83.5 4.4 dynamic-slice_select_fusion.1
  87.8 0.0 all-gather.5.cloned.1.call-update
  87.9 0.0 all-gather.7.cloned.1.call-start
  87.9 0.7 all-gather.7.cloned.1.call-update
  88.6 0.0 reduce-scatter.3.cloned.1.call-start
  88.7 109.1 %all-gather.5.cloned.1.call-done = bf16[8192,512]{1,0:T(8,128)(2,1)} async-done(((bf16[1024,512]{1,0:T(8,128)(2,1)}), bf16[8192,512]{1,0:T(8,128)(2,1)}) %all-gather.5.cloned.1.call-update) | async-done | bytes 8388624 | tf_op jit(solution)/shard_map/all_gather | solution.py:12
  197.7 5.2 reduce_sum.24
  203.0 15.8 %fusion.3 = f32[512,8192]{1,0:T(8,128)} fusion(bf16[1024,512]{1,0:T(8,128)(2,1)S(1)} %reduce_sum.24, bf16[1024,8192]{1,0:T(8,128)(2,1)} %mul.27), kind=kOutput, calls=%fused_computation.8 | convolution fusion | flops 8589934592 | bytes 34603008 | tf_op jit(solution)/shard_map/dot_general | solution.py:30
  218.8 0.0 reduce-scatter.3.cloned.1.call-update
  218.8 0.2 reduce-scatter.5.cloned.1.call-start
  219.1 86.1 %all-gather.7.cloned.1.call-done = bf16[8192,512]{1,0:T(8,128)(2,1)} async-done(((bf16[1024,512]{1,0:T(8,128)(2,1)}), bf16[8192,512]{1,0:T(8,128)(2,1)}) %all-gather.7.cloned.1.call-update) | async-done | bytes 8388624 | tf_op jit(solution)/shard_map/all_gather | solution.py:12
  305.1 5.2 reduce_sum.25
  310.4 15.8 %fusion.4 = f32[512,8192]{1,0:T(8,128)} fusion(bf16[1024,512]{1,0:T(8,128)(2,1)S(1)} %reduce_sum.25, bf16[1024,8192]{1,0:T(8,128)(2,1)} %mul.27), kind=kOutput, calls=%fused_computation.9 | convolution fusion | flops 8589934592 | bytes 34603008 | tf_op jit(solution)/shard_map/dot_general | solution.py:30
  326.2 0.0 copy-start
  326.2 0.0 reduce-scatter.5.cloned.1.call-update
  326.2 161.4 %reduce-scatter.3.cloned.1.call-done = f32[32,8192]{1,0:T(8,128)} async-done(((f32[512,8192]{1,0:T(8,128)}), f32[32,8192]{1,0:T(8,128)}) %reduce-scatter.3.cloned.1.call-update) | async-done | bytes 1048592 | tf_op jit(solution)/shard_map/reduce_scatter | solution.py:17
  487.6 183.4 %reduce-scatter.5.cloned.1.call-done = f32[32,8192]{1,0:T(8,128)} async-done(((f32[512,8192]{1,0:T(8,128)}), f32[32,8192]{1,0:T(8,128)}) %reduce-scatter.5.cloned.1.call-update) | async-done | bytes 1048592 | tf_op jit(solution)/shard_map/reduce_scatter | solution.py:17
  671.1 0.0 copy-done
  671.1 3.1 fusion.1
  (1 shorter events, 0.0 us)
Async XLA Ops:
  6.5 191.2 %all-gather.5.cloned.1.call-start = ((), (), s32[]{:S(2)}) async-start(), calls=%async_computation.4 | async-start | bytes 9437184 | tf_op jit(solution)/shard_map/all_gather | solution.py:12
  87.9 217.3 %all-gather.7.cloned.1.call-start = ((), (), s32[]{:S(2)}) async-start(), calls=%async_computation.5 | async-start | bytes 9437184 | tf_op jit(solution)/shard_map/all_gather | solution.py:12
  88.6 399.0 %reduce-scatter.3.cloned.1.call-start = ((), (), s32[]{:S(2)}) async-start(), calls=%async_computation.2 | async-start | bytes 17825792 | tf_op jit(solution)/shard_map/reduce_scatter | solution.py:17
  218.8 452.3 %reduce-scatter.5.cloned.1.call-start = ((), (), s32[]{:S(2)}) async-start(), calls=%async_computation.3 | async-start | bytes 17825792 | tf_op jit(solution)/shard_map/reduce_scatter | solution.py:17
  326.2 344.9 %copy-start = (f32[2,32,8192]{2,1,0:T(8,128)S(1)}, f32[2,32,8192]{2,1,0:T(8,128)}, u32[]{:S(2)}) copy-start(f32[2,32,8192]{2,1,0:T(8,128)} %param.7) | copy-start | bytes 6291460
Sparse Core Ops, SparseCore 0:
  88.0 109.7 all-gather.4
  200.1 105.0 all-gather.6
  307.5 180.0 reduce-scatter.2
  489.9 181.1 reduce-scatter.4
